TPU v7x, 1024 devices: a whole 4x4x32 slice. The times are simulated.
1024 devices in a mesh: occ: 16 (over x_lo, y, core), vir: 64 (over z, x_hi).
Axes of the slice: x: 4 (x_hi: 2, x_lo: 2; x = x_hi * 2 + x_lo), y: 4, z: 32, core: 2. Of those that a mesh axis runs over, the one named last changes fastest.
Arguments:
- amplitudes: bfloat16 [1600, 98304], P('occ', 'vir'), may hold values from -6 to 6
- integrals: bfloat16 [98304, 8192], P('vir', 'occ'), may hold values from -0.078125 to 0.078125
- block_sizes: int32 [64], replicated, may hold values from 1 to 1536, 49152 in all
Outputs:
- residual: float32 [8192, 1600], P(('occ', 'vir'))
Inputs may be any that keep to these rules, and one draw needn't show every extreme that they name: `block_sizes`: block sizes sum to 49152; at least one block is full.
All inputs are finite; a program needn't handle non-finite values.
Results may differ from a plain program's by a relative error of at most 0.0003.
Values may be sent and summed in bfloat16 or wider, within the bound.
A program may use at most 32 MiB of HBM per device.

v0:
```python
import jax
import jax.numpy as jnp
from jax import lax
from jax.sharding import PartitionSpec as P


def on_device(amplitudes, integrals, block_sizes):
    where_vir = lax.axis_index("vir")
    slots = jnp.arange(block_sizes.shape[0], dtype=jnp.int32)
    own_live = jnp.sum(jnp.where(slots == where_vir, block_sizes, 0))
    rows = jnp.arange(integrals.shape[0], dtype=jnp.int32)
    masked = jnp.where((rows < own_live)[:, None], integrals, jnp.zeros_like(integrals))
    gathered = lax.all_gather(amplitudes, "occ", axis=0, tiled=True)
    return lax.psum_scatter(
        lax.dot_general(
            masked, gathered, (((0,), (1,)), ((), ())), preferred_element_type=jnp.float32
        ),
        "vir",
        scatter_dimension=0,
        tiled=True,
    )


def solution(mesh):
    in_specs = (P("occ", "vir"), P("vir", "occ"), P())
    out_specs = P(("occ", "vir"), None)
    return jax.shard_map(
        on_device, mesh=mesh, in_specs=in_specs, out_specs=out_specs, check_vma=False
    )
```

profile of v0, /device:TPU:16, one launch (start us, length us, event | category | flops | bytes accessed | tf_op | source)
XLA Modules:
  0.0 716.5 jit_solution(14740941976896843501)
XLA Ops:
  6.5 0.0 all-gather.3.cloned.1.call-start
  6.5 0.7 all-gather.3.cloned.1.call-update
  7.3 0.0 all-reduce.3.cloned.1.call-start
  7.3 1.3 fusion.4
  8.6 0.7 iota_compare_fusion
  9.3 0.0 copy-start
  9.3 64.7 %all-gather.3.cloned.1.call-done = bf16[16,100,1536]{2,1,0:T(8,128)(2,1)} async-done(((bf16[1,100,1536]{2,1,0:T(8,128)(2,1)}), bf16[16,100,1536]{2,1,0:T(8,128)(2,1)}) %all-gather.3.cloned.1.call-update) | async-done | bytes 4915216 | tf_op jit(solution)/shard_map/all_gather | solution.py:13
  74.0 7.3 %reshape.5 = bf16[1600,1536]{1,0:T(8,128)(2,1)} reshape(bf16[16,100,1536]{2,1,0:T(8,128)(2,1)} %all-gather.3.cloned.1.call-done) | data formatting | bytes 9830400
  81.2 0.0 copy-done
  81.2 7.5 %fusion = f32[512,1600]{1,0:T(8,128)} fusion(bf16[1600,1536]{1,0:T(8,128)(2,1)} %reshape.5, bf16[1536,512]{1,0:T(8,128)(2,1)S(1)} %copy-done, pred[1536]{0:T(1024)(128)(4,1)S(1)} %iota_compare_fusion), kind=kOutput, calls=%fused_computation | convolution fusion | flops 2517368832 | bytes 9766400 | tf_op jit(solution)/shard_map/dot_general | solution.py:15
  88.7 0.0 all-reduce.3.cloned.1.call-update
  88.7 1.3 dynamic-slice
  90.7 617.5 %all-reduce.3.cloned.1.call-done = f32[512,1600]{1,0:T(8,128)} async-done(((f32[512,1600]{1,0:T(8,128)}), f32[512,1600]{1,0:T(8,128)}) %all-reduce.3.cloned.1.call-update) | async-done | bytes 3276816
  708.2 1.4 constant_dynamic-slice_fusion
Async XLA Ops:
  6.5 67.4 %all-gather.3.cloned.1.call-start = ((), (), s32[]{:S(2)}) async-start(), calls=%async_computation | async-start | bytes 5431296 | tf_op jit(solution)/shard_map/all_gather | solution.py:13
  7.3 700.9 %all-reduce.3.cloned.1.call-start = ((), (), s32[]{:S(2)}) async-start(), calls=%async_computation.1 | async-start | bytes 6815744
  9.3 72.0 %copy-start = (bf16[1536,512]{1,0:T(8,128)(2,1)S(1)}, bf16[1536,512]{1,0:T(8,128)(2,1)}, u32[]{:S(2)}) copy-start(bf16[1536,512]{1,0:T(8,128)(2,1)} %param.4) | copy-start | bytes 4718596
Sparse Core Ops, SparseCore 0:
  10.1 63.8 all-gather.2
  88.8 619.3 all-reduce.2
where the time goes:
time: 717 us; the launch traced here: 716 us
  waiting for transfers between devices  683 us (95%)
  between operations  14.1 us (2%)
  local copies, waits for them, and re-layouts  9.97 us (1%)
  matrix products  7.48 us (1%)
    unnamed x3, waiting for transfers between devices  618 us
    all_gather x1, waiting for transfers between devices, on_device(): gathered = lax.all_gather(amplitudes, 'occ', axis=0, tiled=True)  64.7 us
  transfers between devices with their start and end apart: 2, of which 2 were waited for; matrix products, arithmetic and copies ran while one was open for 0% of the time, Pallas kernels for 0%

commit v1 on v0

v1 whole, which is shorter than its diff:
```python
import jax
import jax.numpy as jnp
from jax import lax
from jax.experimental import pallas as pl
from jax.experimental.pallas import tpu as pltpu
from jax.sharding import PartitionSpec as P

MESH = pl.DeviceIdType.MESH
F32, BF16, I16 = jnp.float32, jnp.bfloat16, jnp.int16
NY, NZ, NVIR, NOCC = 4, 32, 64, 16
ROWS, DEPTH, OWN = 100, 1536, 512
MAIN, HALF, TAIL, QUART = 96, 48, 4, 384
SLOTS, MAINS, COLS = 8, 768, 896
STRIDE = 4
STEPS = 16 // STRIDE
ROUND = 12582912.0
LEAST = 1.1e-34
NT = (((1,), (1,)), ((), ()))


def kernel(
    a_hbm, i_hbm, sizes_hbm, o_ref,
    a_ref, i_ref, sizes_ref, sibling, turned, mains, tails, tail_f32, own_tail, rest_f32, rest,
    part, coded, coded_in, scale, scale_in, total, out_q, out_u, raw_q, raw_u, run_q, run_u, ends, end_in,
    ready_m, ready_t, sent, i_sem, x_sem, raw_sem, run_sem, end_sem, load_sem,
):
    occ, vir = lax.axis_index("occ"), lax.axis_index("vir")
    core = lax.rem(occ, 2)
    y = lax.rem(lax.div(occ, 2), NY)
    x_lo = lax.div(occ, 2 * NY)
    z, x_hi = lax.div(vir, 2), lax.rem(vir, 2)

    def at_y(step):
        return lax.rem(y + step + NY, NY)

    def chip(x, yy, c):
        return (x * (2 * NY) + yy * 2 + c, vir)

    def at_z(step):
        return (occ, lax.rem(vir + 2 * step + NVIR, NVIR))

    twin = chip(x_lo, y, 1 - core)
    other_x = 1 - x_lo
    partner = (occ, vir + 1 - 2 * x_hi)
    peers = [twin, partner]
    for n in range(1, STRIDE + 1):
        peers += [at_z(n), at_z(-n)]
    for c in (0, 1):
        peers += [chip(other_x, y, c), chip(x_lo, at_y(1), c), chip(x_lo, at_y(-1), c)]

    barrier = pltpu.get_barrier_semaphore()
    for peer in peers:
        pl.semaphore_signal(barrier, inc=1, device_id=peer, device_id_type=MESH)

    a_load = pltpu.make_async_copy(a_hbm, a_ref, load_sem.at[0])
    i_load = pltpu.make_async_copy(i_hbm, i_ref, load_sem.at[1])
    sizes_load = pltpu.make_async_copy(sizes_hbm, sizes_ref, load_sem.at[2])
    a_load.start()
    i_load.start()
    sizes_load.start()
    a_load.wait()
    last = a_ref[pl.ds(MAIN, TAIL), :].astype(F32)
    for q in range(4):
        tail_f32[pl.ds(TAIL * q, TAIL), :] = last[:, QUART * q : QUART * (q + 1)]
    own_tail[...] = tail_f32[...].astype(BF16)

    pl.semaphore_wait(barrier, len(peers))

    i_copy = pltpu.make_async_remote_copy(
        src_ref=i_ref, dst_ref=sibling, send_sem=i_sem.at[0], recv_sem=i_sem.at[1],
        device_id=twin, device_id_type=MESH,
    )

    def piece(k, h):
        if h == 2:
            return tails.at[k], ready_t.at[k]
        return mains.at[k, pl.ds(HALF * h, HALF)], ready_m.at[k, h]

    def own_piece(h):
        return own_tail if h == 2 else a_ref.at[pl.ds(HALF * h, HALF)]

    def send(n, src, k, h, dev):
        dst, sem = piece(k, h)
        return pltpu.make_async_remote_copy(
            src_ref=src, dst_ref=dst, send_sem=sent.at[n], recv_sem=sem,
            device_id=dev, device_id_type=MESH,
        )

    def arrived(k, h):
        dst, sem = piece(k, h)
        pltpu.make_async_remote_copy(
            src_ref=dst, dst_ref=dst, send_sem=sent.at[0], recv_sem=sem,
            device_id=twin, device_id_type=MESH,
        ).wait_recv()

    def turn(source, c):
        live = sizes_ref[vir]
        for b in range(DEPTH // 256):
            block = source[pl.ds(256 * b, 256), :].astype(F32)
            row = lax.broadcasted_iota(jnp.int32, block.shape, 0) + 256 * b
            block = jnp.where(row < live, block, 0.0)
            turned[c, :, 256 * b : 256 * (b + 1)] = block.T.astype(BF16)

    up, down, far = at_y(1), at_y(-1), at_y(2)
    shapes = {0: [], 1: []}

    def go(role, src, k, h, dev):
        copy = send(len(shapes[role]), src, k, h, dev)
        copy.start()
        shapes[role].append(h)

    def pass_on(role, k, h, dev):
        go(role, piece(k, h)[0], k, h, dev)

    def start_own(role, dests):
        for dev in dests:
            for h in range(3):
                go(role, own_piece(h), 2 * y + core, h, dev)
        i_load.wait()
        i_copy.start()

    def turn_own():
        sizes_load.wait()
        turn(i_ref, core)

    def turn_sibling():
        i_copy.wait_recv()
        turn(sibling, 1 - core)

    @pl.when(core == 0)
    def _():
        start_own(0, [chip(x_lo, up, 0), chip(x_lo, down, 0), chip(other_x, y, 1)])
        for h in range(2):
            mains[2 * y, pl.ds(HALF * h, HALF)] = a_ref[pl.ds(HALF * h, HALF), :]
        tails[2 * y] = own_tail[...]
        turn_own()
        for c in (0, 1):
            for h in (0, 2, 1):
                for src, dev, keep in ((2 * down + c, up, h != 1), (2 * up + c, down, h == 1)):
                    arrived(src, h)
                    if keep:
                        pass_on(0, src, h, chip(x_lo, dev, 0))
        turn_sibling()
        for c in (0, 1):
            for h in (0, 2, 1):
                arrived(2 * far + c, h)
                pass_on(0, 2 * far + c, h, chip(other_x, y, 1))
        for h in range(3):
            arrived(2 * y + 1, h)

    @pl.when(core == 1)
    def _():
        start_own(1, [chip(x_lo, up, 0), chip(x_lo, down, 0), chip(other_x, y, 1), chip(x_lo, y, 0)])
        turn_own()
        for c in (0, 1):
            for h in range(3):
                arrived(2 * y + c, h)
                for dev in (up, down):
                    pass_on(1, 2 * y + c, h, chip(x_lo, dev, 1))
        turn_sibling()
        for dev in (up, down, far):
            for c in (0, 1):
                for h in range(3):
                    arrived(2 * dev + c, h)

    for k in range(SLOTS):
        block = tails[k].astype(F32)
        for q in range(4):
            rest_f32[pl.ds(TAIL * k, TAIL), QUART * q : QUART * (q + 1)] = block[TAIL * q : TAIL * (q + 1), :]
    rest[pl.ds(0, 32), :] = rest_f32[...].astype(BF16)
    rest[pl.ds(32, 96), :] = jnp.zeros((96, DEPTH), BF16)

    def multiply(c, carry):
        lhs = turned[c]
        for rhs, lo, hi in ((mains[...].reshape(MAINS, DEPTH), 0, MAINS), (rest[...], MAINS, COLS)):
            out = lax.dot_general(lhs, rhs, NT, preferred_element_type=F32)
            out = out.reshape(NZ, 2, 8, hi - lo)
            for h in (0, 1):
                part[h, c, :, :, lo:hi] = out[:, h]
        return carry

    lax.fori_loop(0, 2, multiply, 0)

    def plane(i):
        far_by = 16 - lax.div(i + 1, 2)
        return lax.rem(z + jnp.where(lax.rem(i, 2) == 1, far_by, -far_by) + NZ, NZ)

    def at(step):
        return lax.rem(z + step + NZ, NZ)

    away = 1 - x_hi

    def group_copies(g):
        return [
            pltpu.make_async_remote_copy(
                src_ref=src, dst_ref=dst, send_sem=x_sem.at[0, n, g], recv_sem=x_sem.at[1, n, g],
                device_id=partner, device_id_type=MESH,
            )
            for n, (src, dst) in enumerate((
                (scale.at[g], scale_in.at[g]),
                (coded.at[pl.ds(4 * g, 4)], coded_in.at[pl.ds(4 * g, 4)]),
            ))
        ]

    def rounded(values):
        return ((values + ROUND) - ROUND).astype(jnp.int32).astype(I16)

    def encode(g, carry):
        top = jnp.zeros((8, COLS), F32)
        for n in range(4):
            for c in (0, 1):
                top = jnp.maximum(top, jnp.abs(part[away, c, plane(4 * g + n)]))
        top = jnp.maximum(jnp.max(top, axis=0, keepdims=True), LEAST)
        scale[g] = top * (1.0 / 32767.0)
        gain = 32767.0 / top
        for n in range(4):
            i = 4 * g + n
            coded[i] = rounded(jnp.concatenate([part[away, c, plane(i)] for c in (0, 1)], axis=0) * gain)
        for copy in group_copies(g):
            copy.start()
        return carry

    lax.fori_loop(0, 8, encode, 0)

    def towards(side, distance):
        return at_z(distance if side == 0 else -distance)

    def copies_of(src, dst_q, dst_u, sems, dev):
        return [
            pltpu.make_async_remote_copy(
                src_ref=a, dst_ref=b, send_sem=sems(0, n), recv_sem=sems(1, n), device_id=dev, device_id_type=MESH
            )
            for n, (a, b) in enumerate(((out_q.at[src], dst_q), (out_u.at[src], dst_u)))
        ]

    def raw_copies(side, m, j, src):
        return copies_of(
            src, raw_q.at[side, m, j], raw_u.at[side, m, j],
            lambda end, n: raw_sem.at[end, n, side, m, j], towards(side, j + 1),
        )

    def run_copies(side, m, src):
        return copies_of(
            src, run_q.at[side, m], run_u.at[side, m],
            lambda end, n: run_sem.at[end, n, side, m], towards(side, STRIDE),
        )

    def has_run(side, m):
        return not (side == 1 and m == STEPS - 1)

    def pack(here, values):
        top = jnp.maximum(jnp.max(jnp.abs(values), axis=0, keepdims=True), LEAST)
        out_u[here] = top * (1.0 / 32767.0)
        out_q[here] = rounded(values * (32767.0 / top))

    def unpack(q, u):
        return q.astype(jnp.int32).astype(F32) * u

    def start(copies):
        for copy in copies:
            copy.start()

    def finish(copies):
        for copy in copies:
            copy.wait_recv()

    def distance(i):
        far_by = 16 - (i + 1) // 2
        return far_by if i % 2 == 1 else -far_by

    def take(g):
        finish(group_copies(g))
        unit = scale_in[g]
        for n in range(4):
            k = 16 if (g, n) == (0, 0) else distance(4 * g + n)
            here = at(k)
            values = jnp.concatenate([part[x_hi, c, here] for c in (0, 1)], axis=0)
            values = values + unpack(coded_in[4 * g + n], unit)
            side, k = (0, k) if k > 0 else (1, -k)
            if k == 16:
                pack(here, values)
                start(run_copies(0, STEPS - 1, here))
            elif k % STRIDE:
                pack(here, values)
                start(raw_copies(side, k // STRIDE, k % STRIDE - 1, here))
            else:
                total[here] = values

    def step(m):
        for side in (0, 1):
            here = at(STRIDE * m if side == 0 else -STRIDE * m)
            values = total[here]
            for j in range(STRIDE - 1):
                finish(raw_copies(side, m, j, here))
                values = values + unpack(raw_q[side, m, j], raw_u[side, m, j])
            if has_run(side, m):
                finish(run_copies(side, m, here))
                values = values + unpack(run_q[side, m], run_u[side, m])
            if m > 0:
                pack(here, values)
                start(run_copies(side, m - 1, here))
            else:
                total[here] = values

    last_group = {}
    for i in range(32):
        k = abs(distance(i))
        if i > 0 and k % STRIDE == 0:
            last_group[k // STRIDE] = i // 4
    taken = 0
    for m in reversed(range(STEPS)):
        while taken < min(8, last_group[m] + 2):
            take(taken)
            taken += 1
        step(m)

    ends[0] = total[z, pl.ds(0, 8)]
    ends[1] = total[z, pl.ds(8, 8)]
    end_copy = pltpu.make_async_remote_copy(
        src_ref=ends.at[1 - core], dst_ref=end_in, send_sem=end_sem.at[0], recv_sem=end_sem.at[1],
        device_id=twin, device_id_type=MESH,
    )
    end_copy.start()
    mine = ends[core]
    end_copy.wait_recv()
    theirs = end_in[...]

    def spread(block):
        pieces = []
        for k in range(SLOTS):
            pieces.append(block[:, MAIN * k : MAIN * (k + 1)])
            pieces.append(block[:, MAINS + TAIL * k : MAINS + TAIL * (k + 1)])
        return jnp.concatenate(pieces, axis=1)

    mine, theirs = spread(mine), spread(theirs)
    first = lax.rem(core + x_lo, 2) == 0
    o_ref[...] = jnp.concatenate(
        [jnp.where(first, mine, theirs), jnp.where(first, theirs, mine)], axis=1
    )

    for role in (0, 1):

        @pl.when(core == role)
        def _(role=role):
            for n, h in enumerate(shapes[role]):
                send(n, own_piece(h), 0, h, twin).wait_send()

    i_copy.wait_send()
    sends = [group_copies(g) for g in range(8)]
    for side in (0, 1):
        for m in range(STEPS):
            sends += [raw_copies(side, m, j, 0) for j in range(STRIDE - 1)]
            if has_run(side, m):
                sends.append(run_copies(side, m, 0))
    for copies in sends:
        for copy in copies:
            copy.wait_send()
    end_copy.wait_send()


def on_device(amplitudes, integrals, block_sizes):
    hbm = pl.BlockSpec(memory_space=pltpu.HBM)
    return pl.pallas_call(
        kernel,
        out_shape=jax.ShapeDtypeStruct((8, NOCC * ROWS), F32),
        in_specs=[hbm, hbm, hbm],
        out_specs=pl.BlockSpec(memory_space=pltpu.VMEM),
        scratch_shapes=[
            pltpu.VMEM((ROWS, DEPTH), BF16),
            pltpu.VMEM((DEPTH, OWN), BF16),
            pltpu.SMEM((NVIR,), jnp.int32),
            pltpu.VMEM((DEPTH, OWN), BF16),
            pltpu.VMEM((2, OWN, DEPTH), BF16),
            pltpu.VMEM((SLOTS, MAIN, DEPTH), BF16),
            pltpu.VMEM((SLOTS, 16, QUART), BF16),
            pltpu.VMEM((16, QUART), F32),
            pltpu.VMEM((16, QUART), BF16),
            pltpu.VMEM((32, DEPTH), F32),
            pltpu.VMEM((128, DEPTH), BF16),
            pltpu.VMEM((2, 2, NZ, 8, COLS), F32),
            pltpu.VMEM((NZ, 16, COLS), I16),
            pltpu.VMEM((NZ, 16, COLS), I16),
            pltpu.VMEM((8, 1, COLS), F32),
            pltpu.VMEM((8, 1, COLS), F32),
            pltpu.VMEM((NZ, 16, COLS), F32),
            pltpu.VMEM((NZ, 16, COLS), I16),
            pltpu.VMEM((NZ, 1, COLS), F32),
            pltpu.VMEM((2, STEPS, STRIDE - 1, 16, COLS), I16),
            pltpu.VMEM((2, STEPS, STRIDE - 1, 1, COLS), F32),
            pltpu.VMEM((2, STEPS, 16, COLS), I16),
            pltpu.VMEM((2, STEPS, 1, COLS), F32),
            pltpu.VMEM((2, 8, COLS), F32),
            pltpu.VMEM((8, COLS), F32),
            pltpu.SemaphoreType.DMA((SLOTS, 2)),
            pltpu.SemaphoreType.DMA((SLOTS,)),
            pltpu.SemaphoreType.DMA((32,)),
            pltpu.SemaphoreType.DMA((2,)),
            pltpu.SemaphoreType.DMA((2, 2, 8)),
            pltpu.SemaphoreType.DMA((2, 2, 2, STEPS, STRIDE - 1)),
            pltpu.SemaphoreType.DMA((2, 2, 2, STEPS)),
            pltpu.SemaphoreType.DMA((2,)),
            pltpu.SemaphoreType.DMA((3,)),
        ],
        name="ladder",
        cost_estimate=pl.CostEstimate(
            flops=2 * 1024 * DEPTH * COLS, bytes_accessed=2 * DEPTH * (OWN + ROWS), transcendentals=0
        ),
        compiler_params=pltpu.CompilerParams(
            collective_id=0, has_side_effects=True, vmem_limit_bytes=62 * 2**20
        ),
    )(amplitudes, integrals, block_sizes)


def solution(mesh):
    in_specs = (P("occ", "vir"), P("vir", "occ"), P())
    out_specs = P(("occ", "vir"), None)
    return jax.shard_map(
        on_device, mesh=mesh, in_specs=in_specs, out_specs=out_specs, check_vma=False
    )
```

time: 717 us -> 85.9 us (0.12)
  the two profiles are of different devices: /device:TPU:16 before, /device:TPU:1 now
where the time goes in v1:
time: 85.9 us; the launch traced here: 85.7 us
  Pallas kernels  84.3 us (98%)
  local copies, waits for them, and re-layouts  1.43 us (2%)
    pallas_call x1, Pallas kernels, on_device(): pl.pallas_call(kernel, out_shape=jax.ShapeDtypeStruct((8, NOCC * ROWS), F...  84.3 us

profile of v1, /device:TPU:1, one launch (start us, length us, event | category | flops | bytes accessed | tf_op | source)
XLA Modules:
  0.0 85.7 jit_solution(8768468144243363813)
XLA Ops:
  0.0 84.3 %ladder.1 = f32[8,1600]{1,0:T(8,128)} custom-call(bf16[100,1536]{1,0:T(8,128)(2,1)} %a_hbm.1, bf16[1536,512]{1,0:T(8,128)(2,1)} %i_hbm.1, s32[64]{0:T(128)} %sizes_hbm.1), custom_call_target="tpu_custom_call" | custom-call | flops 2818572288 | bytes 1880064 | tf_op jit(solution)/shard_map/ladder/pallas_call | solution.py:363
  84.3 1.4 %copy.5 = f32[8,1600]{1,0:T(8,128)} copy(f32[8,1600]{1,0:T(8,128)} %ladder.1) | data formatting | bytes 102400

commit v2 on v1

--- a/solution.py
+++ b/solution.py
@@ -42,11 +42,13 @@
     twin = chip(x_lo, y, 1 - core)
     other_x = 1 - x_lo
     partner = (occ, vir + 1 - 2 * x_hi)
-    peers = [twin, partner]
-    for n in range(1, STRIDE + 1):
+    peers = []
+    for n in (STRIDE, 2, 1):
         peers += [at_z(n), at_z(-n)]
+    peers.append(partner)
     for c in (0, 1):
         peers += [chip(other_x, y, c), chip(x_lo, at_y(1), c), chip(x_lo, at_y(-1), c)]
+    peers.append(twin)
 
     barrier = pltpu.get_barrier_semaphore()
     for peer in peers:
@@ -99,7 +101,9 @@
             block = source[pl.ds(256 * b, 256), :].astype(F32)
             row = lax.broadcasted_iota(jnp.int32, block.shape, 0) + 256 * b
             block = jnp.where(row < live, block, 0.0)
-            turned[c, :, 256 * b : 256 * (b + 1)] = block.T.astype(BF16)
+            block = block.T.reshape(NZ, 2, 8, 256)
+            for h in (0, 1):
+                turned[h, c, :, 256 * b : 256 * (b + 1)] = block[:, h].reshape(OWN // 2, 256).astype(BF16)
 
     up, down, far = at_y(1), at_y(-1), at_y(2)
     shapes = {0: [], 1: []}
@@ -170,16 +174,11 @@
     rest[pl.ds(0, 32), :] = rest_f32[...].astype(BF16)
     rest[pl.ds(32, 96), :] = jnp.zeros((96, DEPTH), BF16)
 
-    def multiply(c, carry):
-        lhs = turned[c]
+    def multiply(h):
+        lhs = turned[h].reshape(OWN, DEPTH)
         for rhs, lo, hi in ((mains[...].reshape(MAINS, DEPTH), 0, MAINS), (rest[...], MAINS, COLS)):
             out = lax.dot_general(lhs, rhs, NT, preferred_element_type=F32)
-            out = out.reshape(NZ, 2, 8, hi - lo)
-            for h in (0, 1):
-                part[h, c, :, :, lo:hi] = out[:, h]
-        return carry
-
-    lax.fori_loop(0, 2, multiply, 0)
+            part[h, :, :, :, lo:hi] = out.reshape(2, NZ, 8, hi - lo)
 
     def plane(i):
         far_by = 16 - lax.div(i + 1, 2)
@@ -189,6 +188,7 @@
         return lax.rem(z + step + NZ, NZ)
 
     away = 1 - x_hi
+    multiply(away)
 
     def group_copies(g):
         return [
@@ -221,6 +221,7 @@
         return carry
 
     lax.fori_loop(0, 8, encode, 0)
+    multiply(x_hi)
 
     def towards(side, distance):
         return at_z(distance if side == 0 else -distance)
@@ -236,7 +237,7 @@
     def raw_copies(side, m, j, src):
         return copies_of(
             src, raw_q.at[side, m, j], raw_u.at[side, m, j],
-            lambda end, n: raw_sem.at[end, n, side, m, j], towards(side, j + 1),
+            lambda end, n: raw_sem.at[end, n, side, m, j], towards(side, 2 if j == 1 else 1),
         )
 
     def run_copies(side, m, src):
@@ -280,17 +281,25 @@
             if k == 16:
                 pack(here, values)
                 start(run_copies(0, STEPS - 1, here))
-            elif k % STRIDE:
+            elif k % 2:
                 pack(here, values)
                 start(raw_copies(side, k // STRIDE, k % STRIDE - 1, here))
             else:
                 total[here] = values
 
+    def middle(m):
+        for side in (0, 1):
+            k = STRIDE * m + 2
+            here = at(k if side == 0 else -k)
+            finish(raw_copies(side, m, 2, here))
+            pack(here, total[here] + unpack(raw_q[side, m, 2], raw_u[side, m, 2]))
+            start(raw_copies(side, m, 1, here))
+
     def step(m):
         for side in (0, 1):
             here = at(STRIDE * m if side == 0 else -STRIDE * m)
             values = total[here]
-            for j in range(STRIDE - 1):
+            for j in (0, 1):
                 finish(raw_copies(side, m, j, here))
                 values = values + unpack(raw_q[side, m, j], raw_u[side, m, j])
             if has_run(side, m):
@@ -302,17 +311,8 @@
             else:
                 total[here] = values
 
-    last_group = {}
-    for i in range(32):
-        k = abs(distance(i))
-        if i > 0 and k % STRIDE == 0:
-            last_group[k // STRIDE] = i // 4
-    taken = 0
-    for m in reversed(range(STEPS)):
-        while taken < min(8, last_group[m] + 2):
-            take(taken)
-            taken += 1
-        step(m)
+    for what in ("t0", "t1", "m3", "t2", "s3", "t3", "m2", "t4", "s2", "t5", "m1", "t6", "s1", "t7", "m0", "s0"):
+        {"t": take, "m": middle, "s": step}[what[0]](int(what[1]))
 
     ends[0] = total[z, pl.ds(0, 8)]
     ends[1] = total[z, pl.ds(8, 8)]
@@ -370,7 +370,7 @@
             pltpu.VMEM((DEPTH, OWN), BF16),
             pltpu.SMEM((NVIR,), jnp.int32),
             pltpu.VMEM((DEPTH, OWN), BF16),
-            pltpu.VMEM((2, OWN, DEPTH), BF16),
+            pltpu.VMEM((2, 2, OWN // 2, DEPTH), BF16),
             pltpu.VMEM((SLOTS, MAIN, DEPTH), BF16),
             pltpu.VMEM((SLOTS, 16, QUART), BF16),
             pltpu.VMEM((16, QUART), F32),

time: 85.9 us -> 82.3 us (0.958); the launches traced: 85.7 us -> 81.2 us
  Pallas kernels: 84.3 us -> 79.7 us
    pallas_call x1, Pallas kernels: 84.3 us -> 79.7 us  [on_device(): pl.pallas_call(kernel, out_shape=jax.ShapeDtypeStruct((8, NOCC * ROWS), F...]
where the time goes in v2:
time: 82.3 us; the launch traced here: 81.2 us
  Pallas kernels  79.7 us (97%)
  local copies, waits for them, and re-layouts  1.43 us (2%)
    pallas_call x1, Pallas kernels, on_device(): pl.pallas_call(kernel, out_shape=jax.ShapeDtypeStruct((8, NOCC * ROWS), F...  79.7 us

profile of v2, /device:TPU:1, one launch (start us, length us, event | category | flops | bytes accessed | tf_op | source)
XLA Modules:
  0.0 81.2 jit_solution(3031498714741987610)
XLA Ops:
  0.0 79.7 %ladder.1 = f32[8,1600]{1,0:T(8,128)} custom-call(bf16[100,1536]{1,0:T(8,128)(2,1)} %a_hbm.1, bf16[1536,512]{1,0:T(8,128)(2,1)} %i_hbm.1, s32[64]{0:T(128)} %sizes_hbm.1), custom_call_target="tpu_custom_call" | custom-call | flops 2818572288 | bytes 1880064 | tf_op jit(solution)/shard_map/ladder/pallas_call | solution.py:363
  79.7 1.4 %copy.5 = f32[8,1600]{1,0:T(8,128)} copy(f32[8,1600]{1,0:T(8,128)} %ladder.1) | data formatting | bytes 102400

commit v3 on v2

--- a/solution.py
+++ b/solution.py
@@ -11,6 +11,7 @@
 ROWS, DEPTH, OWN = 100, 1536, 512
 MAIN, HALF, TAIL, QUART = 96, 48, 4, 384
 SLOTS, MAINS, COLS = 8, 768, 896
+PER, GROUPS = 2, 16
 STRIDE = 4
 STEPS = 16 // STRIDE
 ROUND = 12582912.0
@@ -43,7 +44,7 @@
     other_x = 1 - x_lo
     partner = (occ, vir + 1 - 2 * x_hi)
     peers = []
-    for n in (STRIDE, 2, 1):
+    for n in (STRIDE, 3, 2, 1):
         peers += [at_z(n), at_z(-n)]
     peers.append(partner)
     for c in (0, 1):
@@ -198,7 +199,7 @@
             )
             for n, (src, dst) in enumerate((
                 (scale.at[g], scale_in.at[g]),
-                (coded.at[pl.ds(4 * g, 4)], coded_in.at[pl.ds(4 * g, 4)]),
+                (coded.at[pl.ds(PER * g, PER)], coded_in.at[pl.ds(PER * g, PER)]),
             ))
         ]
 
@@ -207,20 +208,20 @@
 
     def encode(g, carry):
         top = jnp.zeros((8, COLS), F32)
-        for n in range(4):
+        for n in range(PER):
             for c in (0, 1):
-                top = jnp.maximum(top, jnp.abs(part[away, c, plane(4 * g + n)]))
+                top = jnp.maximum(top, jnp.abs(part[away, c, plane(PER * g + n)]))
         top = jnp.maximum(jnp.max(top, axis=0, keepdims=True), LEAST)
         scale[g] = top * (1.0 / 32767.0)
         gain = 32767.0 / top
-        for n in range(4):
-            i = 4 * g + n
+        for n in range(PER):
+            i = PER * g + n
             coded[i] = rounded(jnp.concatenate([part[away, c, plane(i)] for c in (0, 1)], axis=0) * gain)
         for copy in group_copies(g):
             copy.start()
         return carry
 
-    lax.fori_loop(0, 8, encode, 0)
+    lax.fori_loop(0, GROUPS, encode, 0)
     multiply(x_hi)
 
     def towards(side, distance):
@@ -237,7 +238,7 @@
     def raw_copies(side, m, j, src):
         return copies_of(
             src, raw_q.at[side, m, j], raw_u.at[side, m, j],
-            lambda end, n: raw_sem.at[end, n, side, m, j], towards(side, 2 if j == 1 else 1),
+            lambda end, n: raw_sem.at[end, n, side, m, j], towards(side, 3 if (m, j) == (3, 2) else 2 if j == 1 else 1),
         )
 
     def run_copies(side, m, src):
@@ -272,16 +273,16 @@
     def take(g):
         finish(group_copies(g))
         unit = scale_in[g]
-        for n in range(4):
-            k = 16 if (g, n) == (0, 0) else distance(4 * g + n)
+        for n in range(PER):
+            k = 16 if (g, n) == (0, 0) else distance(PER * g + n)
             here = at(k)
             values = jnp.concatenate([part[x_hi, c, here] for c in (0, 1)], axis=0)
-            values = values + unpack(coded_in[4 * g + n], unit)
+            values = values + unpack(coded_in[PER * g + n], unit)
             side, k = (0, k) if k > 0 else (1, -k)
             if k == 16:
                 pack(here, values)
                 start(run_copies(0, STEPS - 1, here))
-            elif k % 2:
+            elif k % 2 or k == 14:
                 pack(here, values)
                 start(raw_copies(side, k // STRIDE, k % STRIDE - 1, here))
             else:
@@ -299,7 +300,7 @@
         for side in (0, 1):
             here = at(STRIDE * m if side == 0 else -STRIDE * m)
             values = total[here]
-            for j in (0, 1):
+            for j in range(3 if m == 3 else 2):
                 finish(raw_copies(side, m, j, here))
                 values = values + unpack(raw_q[side, m, j], raw_u[side, m, j])
             if has_run(side, m):
@@ -311,8 +312,11 @@
             else:
                 total[here] = values
 
-    for what in ("t0", "t1", "m3", "t2", "s3", "t3", "m2", "t4", "s2", "t5", "m1", "t6", "s1", "t7", "m0", "s0"):
-        {"t": take, "m": middle, "s": step}[what[0]](int(what[1]))
+    plan = [(take, n) for n in range(GROUPS)]
+    for at_group, what in ((15, (step, 0)), (15, (middle, 0)), (14, (step, 1)), (11, (middle, 1)), (10, (step, 2)), (7, (middle, 2)), (5, (step, 3))):
+        plan.insert(at_group + 1, what)
+    for action, n in plan:
+        action(n)
 
     ends[0] = total[z, pl.ds(0, 8)]
     ends[1] = total[z, pl.ds(8, 8)]
@@ -346,7 +350,7 @@
                 send(n, own_piece(h), 0, h, twin).wait_send()
 
     i_copy.wait_send()
-    sends = [group_copies(g) for g in range(8)]
+    sends = [group_copies(g) for g in range(GROUPS)]
     for side in (0, 1):
         for m in range(STEPS):
             sends += [raw_copies(side, m, j, 0) for j in range(STRIDE - 1)]
@@ -380,8 +384,8 @@
             pltpu.VMEM((2, 2, NZ, 8, COLS), F32),
             pltpu.VMEM((NZ, 16, COLS), I16),
             pltpu.VMEM((NZ, 16, COLS), I16),
-            pltpu.VMEM((8, 1, COLS), F32),
-            pltpu.VMEM((8, 1, COLS), F32),
+            pltpu.VMEM((GROUPS, 1, COLS), F32),
+            pltpu.VMEM((GROUPS, 1, COLS), F32),
             pltpu.VMEM((NZ, 16, COLS), F32),
             pltpu.VMEM((NZ, 16, COLS), I16),
             pltpu.VMEM((NZ, 1, COLS), F32),
@@ -395,7 +399,7 @@
             pltpu.SemaphoreType.DMA((SLOTS,)),
             pltpu.SemaphoreType.DMA((32,)),
             pltpu.SemaphoreType.DMA((2,)),
-            pltpu.SemaphoreType.DMA((2, 2, 8)),
+            pltpu.SemaphoreType.DMA((2, 2, GROUPS)),
             pltpu.SemaphoreType.DMA((2, 2, 2, STEPS, STRIDE - 1)),
             pltpu.SemaphoreType.DMA((2, 2, 2, STEPS)),
             pltpu.SemaphoreType.DMA((2,)),

time: 82.3 us -> 82.1 us (level); the launches traced: 81.2 us -> 81.9 us
  no operation moved by 1% of the time
where the time goes in v3:
time: 82.1 us; the launch traced here: 81.9 us
  Pallas kernels  80.5 us (98%)
  local copies, waits for them, and re-layouts  1.43 us (2%)
    pallas_call x1, Pallas kernels, on_device(): pl.pallas_call(kernel, out_shape=jax.ShapeDtypeStruct((8, NOCC * ROWS), F...  80.5 us

profile of v3, /device:TPU:1, one launch (start us, length us, event | category | flops | bytes accessed | tf_op | source)
XLA Modules:
  0.0 81.9 jit_solution(16758006848141477963)
XLA Ops:
  0.0 80.5 %ladder.1 = f32[8,1600]{1,0:T(8,128)} custom-call(bf16[100,1536]{1,0:T(8,128)(2,1)} %a_hbm.1, bf16[1536,512]{1,0:T(8,128)(2,1)} %i_hbm.1, s32[64]{0:T(128)} %sizes_hbm.1), custom_call_target="tpu_custom_call" | custom-call | flops 2818572288 | bytes 1880064 | tf_op jit(solution)/shard_map/ladder/pallas_call | solution.py:367
  80.5 1.4 %copy.5 = f32[8,1600]{1,0:T(8,128)} copy(f32[8,1600]{1,0:T(8,128)} %ladder.1) | data formatting | bytes 102400

commit v4 on v3

--- a/solution.py
+++ b/solution.py
@@ -297,12 +297,16 @@
             start(raw_copies(side, m, 1, here))
 
     def step(m):
-        for side in (0, 1):
-            here = at(STRIDE * m if side == 0 else -STRIDE * m)
-            values = total[here]
+        planes = [at(STRIDE * m), at(-STRIDE * m)]
+        sums = []
+        for side, here in enumerate(planes):
+            values = total[here] if m > 0 or side == 0 else jnp.zeros((16, COLS), F32)
             for j in range(3 if m == 3 else 2):
                 finish(raw_copies(side, m, j, here))
                 values = values + unpack(raw_q[side, m, j], raw_u[side, m, j])
+            sums.append(values)
+        for side, here in enumerate(planes):
+            values = sums[side]
             if has_run(side, m):
                 finish(run_copies(side, m, here))
                 values = values + unpack(run_q[side, m], run_u[side, m])
@@ -310,7 +314,9 @@
                 pack(here, values)
                 start(run_copies(side, m - 1, here))
             else:
-                total[here] = values
+                sums[side] = values
+        if m == 0:
+            total[z] = sums[0] + sums[1]
 
     plan = [(take, n) for n in range(GROUPS)]
     for at_group, what in ((15, (step, 0)), (15, (middle, 0)), (14, (step, 1)), (11, (middle, 1)), (10, (step, 2)), (7, (middle, 2)), (5, (step, 3))):

time: 82.1 us -> 80.8 us (0.984); the launches traced: 81.9 us -> 79.7 us
  Pallas kernels: 80.5 us -> 78.3 us
    pallas_call x1, Pallas kernels: 80.5 us -> 78.3 us  [on_device(): pl.pallas_call(kernel, out_shape=jax.ShapeDtypeStruct((8, NOCC * ROWS), F...]
where the time goes in v4:
time: 80.8 us; the launch traced here: 79.7 us
  Pallas kernels  78.3 us (97%)
  local copies, waits for them, and re-layouts  1.43 us (2%)
    pallas_call x1, Pallas kernels, on_device(): pl.pallas_call(kernel, out_shape=jax.ShapeDtypeStruct((8, NOCC * ROWS), F...  78.3 us

profile of v4, /device:TPU:1, one launch (start us, length us, event | category | flops | bytes accessed | tf_op | source)
XLA Modules:
  0.0 79.7 jit_solution(4428967481027811518)
XLA Ops:
  0.0 78.3 %ladder.1 = f32[8,1600]{1,0:T(8,128)} custom-call(bf16[100,1536]{1,0:T(8,128)(2,1)} %a_hbm.1, bf16[1536,512]{1,0:T(8,128)(2,1)} %i_hbm.1, s32[64]{0:T(128)} %sizes_hbm.1), custom_call_target="tpu_custom_call" | custom-call | flops 2818572288 | bytes 1880064 | tf_op jit(solution)/shard_map/ladder/pallas_call | solution.py:373
  78.3 1.4 %copy.5 = f32[8,1600]{1,0:T(8,128)} copy(f32[8,1600]{1,0:T(8,128)} %ladder.1) | data formatting | bytes 102400
